TPU v7x, 512 devices: a whole 4x8x8 slice. The times are simulated.
512 devices in a mesh: row: 32 (over z_lo, y, core), col: 16 (over x, z_hi).
Axes of the slice: x: 4, y: 8, z: 8 (z_hi: 4, z_lo: 2; z = z_hi * 2 + z_lo), core: 2. Of those that a mesh axis runs over, the one named last changes fastest.
Arguments:
- out_inverse: bfloat16 [14336, 14336], P('row', 'col'), may hold values from -1 to 2, as said below
- gradient: bfloat16 [14336, 4096], P('col', 'row'), may hold values from -6 to 6
- in_inverse: bfloat16 [4096, 4096], P('row', 'col'), may hold values from -1 to 2, as said below
Outputs:
- preconditioned: bfloat16 [14336, 4096], P('row', 'col')
Inputs may be any that keep to these rules, and one draw needn't show every extreme that they name: out_inverse is symmetric and positive definite. in_inverse is symmetric and positive definite.
All inputs are finite; a program needn't handle non-finite values.
Results may differ from a plain program's by a relative error of at most 0.02.
Values may be sent and summed in bfloat16 or wider, within the bound.
A program may use at most 64 MiB of HBM per device.

v0:
```python
import jax
import jax.numpy as jnp
from jax import lax
from jax.sharding import PartitionSpec as P


def body(out_inverse, gradient, in_inverse):
    partial_rows = jnp.dot(
        out_inverse,
        lax.all_gather(gradient, "row", axis=1, tiled=True),
        preferred_element_type=jnp.float32,
    ).astype(jnp.bfloat16)
    panel = lax.all_gather(in_inverse, "row", axis=0, tiled=True)
    shares = (
        lax.psum_scatter(partial_rows, "col", scatter_dimension=1, tiled=True)
        .astype(jnp.float32)
        .astype(jnp.bfloat16)
    )
    result = jnp.dot(
        lax.all_gather(shares, "col", axis=1, tiled=True), panel, preferred_element_type=jnp.float32
    )
    return result.astype(jnp.bfloat16)


def solution(mesh):
    in_specs = (P("row", "col"), P("col", "row"), P("row", "col"))
    out_specs = P("row", "col")
    return jax.shard_map(body, mesh=mesh, in_specs=in_specs, out_specs=out_specs, check_vma=False)
```

profile of v0, /device:TPU:1, one launch (start us, length us, event | category | flops | bytes accessed | tf_op | source)
XLA Modules:
  0.0 373.4 jit_solution(9472991472901375582)
XLA Ops:
  6.5 0.0 copy-start
  6.5 0.0 all-gather.4.cloned.1.call-start
  6.5 0.7 all-gather.4.cloned.1.call-update
  7.3 0.0 reduce-scatter.2.cloned.1.call-start
  7.3 96.1 %all-gather.4.cloned.1.call-done = bf16[896,4096]{1,0:T(8,128)(2,1)} async-done(((bf16[896,128]{1,0:T(8,128)(2,1)}), bf16[896,4096]{1,0:T(8,128)(2,1)}) %all-gather.4.cloned.1.call-update) | async-done | bytes 7340048 | tf_op jit(solution)/shard_map/all_gather | solution.py:10
  103.4 0.0 copy-done
  103.4 8.5 %convolution_convert_fusion = bf16[448,4096]{1,0:T(8,128)(2,1)} fusion(bf16[448,896]{1,0:T(8,128)(2,1)S(1)} %copy-done, bf16[896,4096]{1,0:T(8,128)(2,1)} %all-gather.4.cloned.1.call-done), kind=kOutput, calls=%fused_computation | convolution fusion | flops 3290169344 | bytes 11812864 | tf_op jit(solution)/shard_map/dot_general | solution.py:8
  111.9 0.0 reduce-scatter.2.cloned.1.call-update
  112.0 0.0 all-gather.8.cloned.1.call-start
  112.0 0.7 all-gather.8.cloned.1.call-update
  112.7 0.0 all-gather.6.cloned.1.call-start
  112.7 94.5 %reduce-scatter.2.cloned.1.call-done = bf16[448,256]{1,0:T(8,128)(2,1)} async-done(((bf16[448,4096]{1,0:T(8,128)(2,1)}), bf16[448,256]{1,0:T(8,128)(2,1)}) %reduce-scatter.2.cloned.1.call-update) | async-done | bytes 229392 | tf_op jit(solution)/shard_map/reduce_scatter | solution.py:15
  207.2 0.0 all-gather.6.cloned.1.call-update
  207.3 68.9 %all-gather.8.cloned.1.call-done = bf16[4096,256]{1,0:T(8,128)(2,1)} async-done(((bf16[128,256]{1,0:T(8,128)(2,1)}), bf16[4096,256]{1,0:T(8,128)(2,1)}) %all-gather.8.cloned.1.call-update) | async-done | bytes 2097168 | tf_op jit(solution)/shard_map/all_gather | solution.py:13
  276.1 86.3 %all-gather.6.cloned.1.call-done = bf16[448,4096]{1,0:T(8,128)(2,1)} async-done(((bf16[448,256]{1,0:T(8,128)(2,1)}), bf16[448,4096]{1,0:T(8,128)(2,1)}) %all-gather.6.cloned.1.call-update) | async-done | bytes 3670032 | tf_op jit(solution)/shard_map/all_gather | solution.py:20
  362.4 4.5 %convolution_convert_fusion.1 = bf16[448,256]{1,0:T(8,128)(2,1)} fusion(bf16[448,4096]{1,0:T(8,128)(2,1)} %all-gather.6.cloned.1.call-done, bf16[4096,256]{1,0:T(8,128)(2,1)} %all-gather.8.cloned.1.call-done), kind=kOutput, calls=%fused_computation.1 | convolution fusion | flops 939638784 | bytes 5996544 | tf_op jit(solution)/shard_map/dot_general | solution.py:19
Async XLA Ops:
  6.5 96.9 %copy-start = (bf16[448,896]{1,0:T(8,128)(2,1)S(1)}, bf16[448,896]{1,0:T(8,128)(2,1)}, u32[]{:S(2)}) copy-start(bf16[448,896]{1,0:T(8,128)(2,1)} %param.3) | copy-start | bytes 2408452
  6.5 96.9 %all-gather.4.cloned.1.call-start = ((), (), s32[]{:S(2)}) async-start(), calls=%async_computation.1 | async-start | bytes 7569408 | tf_op jit(solution)/shard_map/all_gather | solution.py:10
  7.3 200.0 %reduce-scatter.2.cloned.1.call-start = ((), (), s32[]{:S(2)}) async-start(), calls=%async_computation.2 | async-start | bytes 3899392 | tf_op jit(solution)/shard_map/reduce_scatter | solution.py:15
  112.0 164.2 %all-gather.8.cloned.1.call-start = ((), (), s32[]{:S(2)}) async-start(), calls=%async_computation.4 | async-start | bytes 2162688 | tf_op jit(solution)/shard_map/all_gather | solution.py:13
  112.7 249.7 %all-gather.6.cloned.1.call-start = ((), (), s32[]{:S(2)}) async-start(), calls=%async_computation.3 | async-start | bytes 3899392 | tf_op jit(solution)/shard_map/all_gather | solution.py:20
Sparse Core Ops, SparseCore 0:
  9.4 93.9 all-gather.3
  112.1 95.1 reduce-scatter.1
  209.4 66.6 all-gather.7
  279.0 83.3 all-gather.5
where the time goes:
time: 374 us; the launch traced here: 373 us
  waiting for transfers between devices  347 us (93%)
  between operations  13.1 us (4%)
  matrix products  13 us (3%)
    all_gather x1, waiting for transfers between devices, body(): lax.all_gather(gradient, 'row', axis=1, tiled=True)  96.1 us
    reduce_scatter x1, waiting for transfers between devices, body(): lax.psum_scatter(partial_rows, 'col', scatter_dimension=1, tiled=True)  94.5 us
    all_gather x1, waiting for transfers between devices, body(): lax.all_gather(shares, 'col', axis=1, tiled=True)  86.3 us
    all_gather x1, waiting for transfers between devices, body(): panel = lax.all_gather(in_inverse, 'row', axis=0, tiled=True)  68.9 us
    dot_general x1, matrix products, body(): jnp.dot(out_inverse, lax.all_gather(gradient, 'row', axis=1, tiled=True),...  8.53 us
  transfers between devices with their start and end apart: 4, of which 4 were waited for; matrix products, arithmetic and copies ran while one was open for 0% of the time, Pallas kernels for 0%

commit v1 on v0

v1 whole, which is shorter than its diff:
```python
import jax
import jax.numpy as jnp
from jax import lax
from jax.experimental import pallas as pl
from jax.experimental.pallas import tpu as pltpu
from jax.sharding import PartitionSpec as P

MESH = pl.DeviceIdType.MESH
BF16 = jnp.bfloat16
F32 = jnp.float32
RY, RX, RZ = 8, 4, 4
ROWS, HALF, QUARTER, LANES = 448, 224, 112, 128
STEPS = ((0,), (7, 1), (6, 2), (5, 3), (4,))
NEAR_Z = (0, 1, 7, 2, 6, 3, 5, 4)
NEAR_ZH = (0, 1, 3, 2)
FAR_FIRST = ((0, 0), (1, 2), (0, 1), (1, 3), (0, 2), (1, 0), (0, 3), (1, 1))


def rem(a, b):
    return lax.rem(a, jnp.int32(b))


def div(a, b):
    return lax.div(a, jnp.int32(b))


def kernel(
    a_ref, g_ref, b_ref, out_ref,
    a_all, g_all, b_own, b_turned, b_all, f_part, c_out, c_in, z_out, z_in, h_all, part, relayed, x_in, x_sum, z_part, z_sum,
    loc, g_s, g_r, h_s, h_r, bz_s, bz_r, bm_s, bm_r, bp_s, bp_r, a_s, a_r, c_s, c_r, z_s, z_r,
    x_s, rel_r, x_r, zz_s, zz_r, last_s, last_r,
):
    row, col = lax.axis_index("row"), lax.axis_index("col")
    core = rem(row, 2)
    y = rem(div(row, 2), RY)
    zl = div(row, 2 * RY)
    x, zh = div(col, RZ), rem(col, RZ)
    own = zl * 2 + core

    def device(zl_=zl, y_=y, core_=core, x_=x, zh_=zh):
        return ((zl_ * RY + y_) * 2 + core_, x_ * RZ + zh_)

    y_to = (device(y_=rem(y + 1, RY)), device(y_=rem(y + RY - 1, RY)))
    x_up, x_down = device(x_=rem(x + 1, RX)), device(x_=rem(x + RX - 1, RX))
    core_other, zl_other = device(core_=1 - core), device(zl_=1 - zl)
    x_pair, x_mirror = device(x_=x + 1 - 2 * rem(x, 2)), device(x_=RX - 1 - x)

    def remote(src, dst, send, recv, to):
        return pltpu.make_async_remote_copy(
            src_ref=src, dst_ref=dst, send_sem=send, recv_sem=recv, device_id=to, device_id_type=MESH
        )

    def send(src, dst, s, r, to):
        remote(src, dst, s, r, to).start()

    def sent(src, s):
        remote(src, src, s, s, core_other).wait_send()

    def arrived(dst, r):
        remote(dst, dst, r, r, core_other).wait_recv()

    loads = [
        pltpu.make_async_copy(g_ref, g_all.at[y], loc.at[0]),
        pltpu.make_async_copy(b_ref.at[:, pl.ds(0, LANES)], b_own.at[0], loc.at[1]),
        pltpu.make_async_copy(b_ref.at[:, pl.ds(LANES, LANES)], b_own.at[1], loc.at[2]),
        pltpu.make_async_copy(a_ref, a_all.at[own], loc.at[3]),
    ]
    for load in loads:
        load.start()
    barrier = pltpu.get_barrier_semaphore()
    place = (zh * 2 + zl) * 2 + core
    for step in range(1, 16):
        there = rem(place + step, 16)
        pl.semaphore_signal(
            barrier,
            inc=1,
            device_id=device(zl_=rem(div(there, 2), 2), core_=rem(there, 2), zh_=div(there, 4)),
            device_id_type=MESH,
        )
    for to in (*y_to, x_up, x_down):
        pl.semaphore_signal(barrier, inc=1, device_id=to, device_id_type=MESH)
    from_zl = 1 - rem(div(x, 2) + rem(zh, 2), 2)
    from_x = rem(x + 2 * core + 1 - zl, RX)

    def from_here(half, q):
        return (x == from_x) & (zl == from_zl) & (core == half) & (zh == q)

    for half in range(2):
        for q in range(RZ):

            @pl.when(jnp.logical_not(from_here(half, q)))
            def _():
                pl.semaphore_signal(
                    barrier,
                    inc=1,
                    device_id=device(zl_=from_zl, core_=jnp.int32(half), x_=from_x, zh_=jnp.int32(q)),
                    device_id_type=MESH,
                )

    for load in loads:
        load.wait()
    for h in range(2):
        b_turned[h] = b_own[h].astype(F32).T.astype(BF16)
    pl.semaphore_wait(barrier, 27 - jnp.where((x == from_x) & (zl == from_zl), 1, 0))

    def ring_part(buf, owner, i):
        return buf.at[owner, pl.ds(i * HALF, HALF)]

    def ring_send(buf, s, r, way, hop, i):
        owner = rem(y + (RY - hop if way == 0 else hop), RY)
        send(ring_part(buf, owner, i), ring_part(buf, owner, i), s.at[way, hop, i], r.at[way, hop, i], y_to[way])

    def ring_wait(buf, r, way, hop, i):
        owner = rem(y + (RY - hop - 1 if way == 0 else hop + 1), RY)
        arrived(ring_part(buf, owner, i), r.at[way, hop, i])

    def ring_hop(buf, s, r, hop):
        for way, i in FAR_FIRST:
            ring_wait(buf, r, way, hop - 1, i)
            if hop < 3 or i // 2 == way:
                ring_send(buf, s, r, way, hop, i)

    def ring_end(buf, r):
        for way, i in FAR_FIRST:
            if i // 2 == way:
                ring_wait(buf, r, way, 3, i)

    def ring_sent(buf, s):
        for way, i in FAR_FIRST:
            for hop in range(4):
                if hop < 3 or i // 2 == way:
                    sent(ring_part(buf, 0, i), s.at[way, hop, i])

    for way, i in FAR_FIRST:
        ring_send(g_all, g_s, g_r, way, 0, i)

    b_here = rem(x, 2) * 4
    b_zl = div(x, 2)

    b_source = zl == b_zl
    b_first = rem(rem(x, 2) + rem(b_zl + zl, 2), 2) * 4

    for e in NEAR_ZH:
        to_zh = rem(zh + e, RZ)
        for h in range(2):

            def away():
                send(
                    b_turned.at[h], b_all.at[b_here + zh, own], bz_s.at[h, e], bz_r.at[own, zh],
                    device(zl_=b_zl, core_=jnp.int32(h), zh_=to_zh),
                )

            if e == 0:

                @pl.when(b_source & (core == h))
                def _():
                    b_all[b_here + zh, own] = b_turned[h]

                pl.when(jnp.logical_not(b_source & (core == h)))(away)
            else:
                away()

    def chunk(half, i):
        there = rem(2 * zh + zl + NEAR_Z[i], 2 * RZ)
        return b_all.at[half + div(there, 2), pl.ds(2 * rem(there, 2), 2)]

    def b_start(first, last):
        @pl.when(b_source)
        def _():
            for i in range(first, last):
                there = rem(2 * zh + zl + NEAR_Z[i], 2 * RZ)
                for c in range(2) if i > 0 else (1 - core,):
                    s = 2 * rem(there, 2) + c
                    arrived(b_all.at[b_here + div(there, 2), s], bz_r.at[s, div(there, 2)])
                block = chunk(b_here, i)
                send(block, block, bm_s.at[i], bm_r.at[i], x_mirror)
                send(block, block, bp_s.at[i], bp_r.at[i], x_pair)

    def b_forward(first, last):
        @pl.when(jnp.logical_not(b_source))
        def _():
            for i in range(first, last):
                block = chunk(b_first, i)
                arrived(block, bm_r.at[i])
                send(block, block, bp_s.at[i], bp_r.at[i], x_pair)

    b_start(0, 3)
    ring_hop(g_all, g_s, g_r, 1)
    b_start(3, 8)
    send(a_all.at[own], a_all.at[own], a_s.at[0], a_r.at[0], zl_other)
    send(a_all.at[own], a_all.at[own], a_s.at[1], a_r.at[1], core_other)
    b_forward(0, 3)
    ring_hop(g_all, g_s, g_r, 2)
    b_forward(3, 8)
    ring_hop(g_all, g_s, g_r, 3)
    ring_end(g_all, g_r)
    for i in range(2 * RZ):
        arrived(chunk(4 - b_first, i), bp_r.at[i])

    mine = rem(zl + y, 2)
    right = jnp.concatenate([b_all[:, t].reshape(RY * LANES, LANES) for t in range(4)], axis=1)
    for m in range(5):
        if m < 4:
            rows = pl.ds(m * HALF, HALF)
            left = jnp.concatenate([g_all[j, rows] for j in range(RY)], axis=1)
            share = jnp.dot(left, right, preferred_element_type=F32)
            for t in range(4):
                f_part[m, t] = share[:, t * LANES : (t + 1) * LANES]
            for t in range(2):
                c_out[m, t] = f_part[m, 2 * t + 1 - core].astype(BF16)
            send(c_out.at[m], c_in.at[m], c_s.at[m], c_r.at[m], core_other)
        if m >= 1:
            arrived(c_in.at[m - 1], c_r.at[m - 1])
            z_out[m - 1] = (
                f_part[m - 1, 2 * (1 - mine) + core] + c_in[m - 1, 1 - mine].astype(F32)
            ).astype(BF16)
            send(z_out.at[m - 1], z_in.at[m - 1], z_s.at[m - 1], z_r.at[m - 1], zl_other)
    a_next = a_all.at[2 * (1 - zl) + core]
    arrived(a_next, a_r.at[0])
    send(a_next, a_next, a_s.at[2], a_r.at[2], core_other)
    for m in range(4):
        arrived(z_in.at[m], z_r.at[m])
        h_all[y, pl.ds(m * HALF, HALF)] = (
            f_part[m, 2 * mine + core] + c_in[m, mine].astype(F32) + z_in[m].astype(F32)
        ).astype(BF16)
        for way in range(2):
            ring_send(h_all, h_s, h_r, way, 0, m)
    arrived(a_all.at[2 * zl + 1 - core], a_r.at[1])
    arrived(a_all.at[2 * (1 - zl) + 1 - core], a_r.at[2])

    def owner_x(o, plane):
        yy = rem(y + o, RY)
        return 2 * rem(plane + yy, 2) + div(yy, 4)

    def rows_at(o, at_x):
        away = rem(at_x + RX - owner_x(o, zl), RX)
        return 2 * (1 - rem(away, 2)) + div(away, 2)

    def multiply(step, s):
        offsets = STEPS[step]
        right = jnp.concatenate([h_all[rem(y + o, RY)] for o in offsets], axis=1)
        product = jnp.dot(a_all[s], right, preferred_element_type=F32).astype(BF16)
        for i, o in enumerate(offsets):
            to_x = rem(owner_x(o, zl) + 2 * rem(s, 2) + 1 - div(s, 2), RX)
            for half in range(2):
                part[step, to_x, half, i] = product[half * HALF : (half + 1) * HALF, i * LANES : (i + 1) * LANES]

    def count(step):
        return pl.ds(0, len(STEPS[step]))

    s_up, s_down, s_far = rem(x + 1, RX), rem(x + RX - 1, RX), rem(x + 2, RX)

    def x_send(step):
        n = count(step)
        if len(STEPS[step]) == 1:
            o = STEPS[step][0]
            multiply(step, rows_at(o, s_far))
        else:
            lax.fori_loop(0, 4, lambda i, carry: (multiply(step, i), carry)[1], 0)
        send(part.at[step, s_far, 0, n], relayed.at[step, 0, n], x_s.at[step, 0], rel_r.at[step, 0], x_down)
        send(part.at[step, s_far, 1, n], relayed.at[step, 1, n], x_s.at[step, 1], rel_r.at[step, 1], x_up)
        if len(STEPS[step]) == 1:
            lax.fori_loop(3, 6, lambda i, carry: (multiply(step, rows_at(o, rem(x + i, RX))), carry)[1], 0)
        send(part.at[step, s_down, 1, n], x_in.at[step, 0, 1, n], x_s.at[step, 2], x_r.at[step, 0, 1], x_down)
        send(part.at[step, s_up, 0, n], x_in.at[step, 1, 0, n], x_s.at[step, 3], x_r.at[step, 1, 0], x_up)

    def x_relay(step):
        n = count(step)
        for half, s, to in ((0, s_down, x_down), (1, s_up, x_up)):
            arrived(relayed.at[step, half, n], rel_r.at[step, half])
            for i in range(len(STEPS[step])):
                part[step, s, half, i] = (
                    part[step, s, half, i].astype(F32) + relayed[step, half, i].astype(F32)
                ).astype(BF16)
            send(
                part.at[step, s, half, n], x_in.at[step, half, half, n], x_s.at[step, 4 + half],
                x_r.at[step, half, half], to,
            )

    def z_send(step):
        n = count(step)
        for half in range(2):
            for side in range(2):
                arrived(x_in.at[step, side, half, n], x_r.at[step, side, half])
            for i in range(len(STEPS[step])):
                total = (
                    part[step, x, half, i].astype(F32)
                    + x_in[step, 0, half, i].astype(F32)
                    + x_in[step, 1, half, i].astype(F32)
                ).astype(BF16)
                for q in range(2):
                    x_sum[step, 2 * half + q, i] = total[q * QUARTER : (q + 1) * QUARTER]
            for q in range(2 * half, 2 * half + 2):
                send(
                    x_sum.at[step, q, n], z_part.at[step, zh, n], zz_s.at[step, q], zz_r.at[step, zh],
                    device(zl_=1 - zl, zh_=jnp.int32(q)),
                )

    def owner(o):
        to_x = owner_x(o, 1 - zl)
        away = rem(x + RX - to_x, RX)
        return 1 - rem(away, 2), div(away, 2), to_x, rem(rem(y + o, RY), 4)

    def owned_here(o):
        to_zl, to_core, to_x, to_zh = owner(o)
        return (zl == to_zl) & (core == to_core) & (to_x == x) & (to_zh == zh)

    def piece(half, q):
        return out_ref.at[pl.ds(q * QUARTER, QUARTER), pl.ds(pl.multiple_of(half * LANES, LANES), LANES)]

    def last_send(step):
        n = count(step)
        for s in range(RZ):
            arrived(z_part.at[step, s, n], zz_r.at[step, s])
        for i, o in enumerate(STEPS[step]):
            total = z_part[step, 0, i].astype(F32)
            for s in range(1, RZ):
                total = total + z_part[step, s, i].astype(F32)
            z_sum[o] = total.astype(BF16)
            to_zl, to_core, to_x, to_zh = owner(o)

            @pl.when(owned_here(o))
            def _():
                pltpu.make_async_copy(z_sum.at[o], piece(core, zh), last_s.at[o]).start()

            @pl.when(jnp.logical_not(owned_here(o)))
            def _():
                send(
                    z_sum.at[o], piece(core, zh), last_s.at[o], last_r.at[core, zh],
                    device(zl_=to_zl, core_=to_core, x_=to_x, zh_=to_zh),
                )

    for step in range(len(STEPS) + 2):
        if 1 <= step <= 3:
            ring_hop(h_all, h_s, h_r, step)
        if step == 4:
            ring_end(h_all, h_r)
        for stage, back in ((x_send, 0), (x_relay, 0), (z_send, 1), (last_send, 2)):
            if 0 <= step - back < len(STEPS):
                stage(step - back)

    ring_sent(g_all, g_s)
    ring_sent(h_all, h_s)
    for e in NEAR_ZH:
        for h in range(2):

            def left_here():
                sent(b_turned.at[h], bz_s.at[h, e])

            if e == 0:
                pl.when(jnp.logical_not(b_source & (core == h)))(left_here)
            else:
                left_here()

    for i in range(2 * RZ):
        sent(chunk(0, i), bp_s.at[i])

    @pl.when(b_source)
    def _():
        for i in range(2 * RZ):
            sent(chunk(0, i), bm_s.at[i])

    for i in range(3):
        sent(a_all.at[0], a_s.at[i])
    for m in range(4):
        sent(c_out.at[m], c_s.at[m])
        sent(z_out.at[m], z_s.at[m])
    for step in range(len(STEPS)):
        n = count(step)
        for i in range(6):
            sent(part.at[step, 0, 0, n], x_s.at[step, i])
        for q in range(RZ):
            sent(x_sum.at[step, q, n], zz_s.at[step, q])
    for o in range(RY):

        @pl.when(owned_here(o))
        def _():
            pltpu.make_async_copy(z_sum.at[o], piece(core, zh), last_s.at[o]).wait()

        @pl.when(jnp.logical_not(owned_here(o)))
        def _():
            sent(z_sum.at[o], last_s.at[o])

    for half in range(2):
        for q in range(RZ):

            @pl.when(jnp.logical_not(from_here(half, q)))
            def _():
                arrived(piece(jnp.int32(half), jnp.int32(q)), last_r.at[half, q])


def body(out_inverse, gradient, in_inverse):
    dma = pltpu.SemaphoreType.DMA
    vmem = pltpu.VMEM
    return pl.pallas_call(
        kernel,
        out_shape=jax.ShapeDtypeStruct((ROWS, 2 * LANES), BF16),
        in_specs=[pl.BlockSpec(memory_space=pl.ANY)] * 3,
        out_specs=pl.BlockSpec(memory_space=pl.ANY),
        scratch_shapes=[
            vmem((4, ROWS, 2 * ROWS), BF16),
            vmem((RY, 2 * ROWS, LANES), BF16),
            vmem((2, LANES, LANES), BF16),
            vmem((2, LANES, LANES), BF16),
            vmem((RY, 4, LANES, LANES), BF16),
            vmem((4, 4, HALF, LANES), F32),
            vmem((4, 2, HALF, LANES), BF16),
            vmem((4, 2, HALF, LANES), BF16),
            vmem((4, HALF, LANES), BF16),
            vmem((4, HALF, LANES), BF16),
            vmem((RY, 2 * ROWS, LANES), BF16),
            vmem((5, 4, 2, 2, HALF, LANES), BF16),
            vmem((5, 2, 2, HALF, LANES), BF16),
            vmem((5, 2, 2, 2, HALF, LANES), BF16),
            vmem((5, RZ, 2, QUARTER, LANES), BF16),
            vmem((5, RZ, 2, QUARTER, LANES), BF16),
            vmem((RY, QUARTER, LANES), BF16),
            dma((4,)),
            dma((2, 4, 4)), dma((2, 4, 4)),
            dma((2, 4, 4)), dma((2, 4, 4)),
            dma((2, RZ)), dma((4, RZ)),
            dma((2 * RZ,)), dma((2 * RZ,)),
            dma((2 * RZ,)), dma((2 * RZ,)),
            dma((3,)), dma((3,)),
            dma((4,)), dma((4,)),
            dma((4,)), dma((4,)),
            dma((5, 6)), dma((5, 2)), dma((5, 2, 2)),
            dma((5, RZ)), dma((5, RZ)),
            dma((RY,)), dma((2, RZ)),
        ],
        compiler_params=pltpu.CompilerParams(
            collective_id=0, has_side_effects=True, vmem_limit_bytes=64 * 1024 * 1024
        ),
        cost_estimate=pl.CostEstimate(flops=4_300_000_000, bytes_accessed=2_000_000, transcendentals=0),
    )(out_inverse, gradient, in_inverse)


def solution(mesh):
    in_specs = (P("row", "col"), P("col", "row"), P("row", "col"))
    return jax.shard_map(body, mesh=mesh, in_specs=in_specs, out_specs=P("row", "col"), check_vma=False)
```

time: 374 us -> 103 us (0.28)
  the two profiles are of different devices: /device:TPU:1 before, /device:TPU:3 now
where the time goes in v1:
time: 103 us
  Pallas kernels  101 us (98%)
  local copies, waits for them, and re-layouts  1.64 us (2%)
    pallas_call x1, Pallas kernels, body(): pl.pallas_call(kernel, out_shape=jax.ShapeDtypeStruct((ROWS, 2 * LANES),...  101 us

profile of v1, /device:TPU:3, one launch (start us, length us, event | category | flops | bytes accessed | tf_op | source)
XLA Modules:
  0.0 103.1 jit_solution(4397515423081751617)
XLA Ops:
  0.0 101.4 %shard_map.37 = bf16[448,256]{1,0:T(8,128)(2,1)} custom-call(bf16[448,896]{1,0:T(8,128)(2,1)} %a_ref.1, bf16[896,128]{1,0:T(8,128)(2,1)} %g_ref.1, bf16[128,256]{1,0:T(8,128)(2,1)} %b_ref.1), custom_call_target="tpu_custom_call" | custom-call | flops 4300000256 | bytes 2000000 | tf_op jit(solution)/shard_map/pallas_call | solution.py:395
  101.4 1.6 %copy.5 = bf16[448,256]{1,0:T(8,128)(2,1)} copy(bf16[448,256]{1,0:T(8,128)(2,1)} %shard_map.37) | data formatting | bytes 458752

commit v2 on v1

--- a/solution.py
+++ b/solution.py
@@ -125,11 +125,10 @@
             if i // 2 == way:
                 ring_wait(buf, r, way, 3, i)
 
-    def ring_sent(buf, s):
+    def ring_sent(buf, s, hop):
         for way, i in FAR_FIRST:
-            for hop in range(4):
-                if hop < 3 or i // 2 == way:
-                    sent(ring_part(buf, 0, i), s.at[way, hop, i])
+            if hop < 3 or i // 2 == way:
+                sent(ring_part(buf, 0, i), s.at[way, hop, i])
 
     for way, i in FAR_FIRST:
         ring_send(g_all, g_s, g_r, way, 0, i)
@@ -330,47 +329,74 @@
                     device(zl_=to_zl, core_=to_core, x_=to_x, zh_=to_zh),
                 )
 
+    def g_sent():
+        for hop in range(4):
+            ring_sent(g_all, g_s, hop)
+
+    def b_sent():
+        for e in NEAR_ZH:
+            for h in range(2):
+
+                def left_here():
+                    sent(b_turned.at[h], bz_s.at[h, e])
+
+                if e == 0:
+                    pl.when(jnp.logical_not(b_source & (core == h)))(left_here)
+                else:
+                    left_here()
+
+        for i in range(2 * RZ):
+            sent(chunk(0, i), bp_s.at[i])
+
+        @pl.when(b_source)
+        def _():
+            for i in range(2 * RZ):
+                sent(chunk(0, i), bm_s.at[i])
+
+    def a_sent():
+        for i in range(3):
+            sent(a_all.at[0], a_s.at[i])
+        for m in range(4):
+            sent(c_out.at[m], c_s.at[m])
+            sent(z_out.at[m], z_s.at[m])
+        ring_sent(h_all, h_s, 0)
+
+    def steps_sent(step):
+        n = count(step)
+        for i in range(6):
+            sent(part.at[step, 0, 0, n], x_s.at[step, i])
+        for q in range(RZ):
+            sent(x_sum.at[step, q, n], zz_s.at[step, q])
+
+    def all_sent(step):
+        if step == 0:
+            g_sent()
+        elif step == 1:
+            b_sent()
+        elif step == 2:
+            a_sent()
+        else:
+            ring_sent(h_all, h_s, step - 2)
+            steps_sent(step - 3)
+
     for step in range(len(STEPS) + 2):
         if 1 <= step <= 3:
             ring_hop(h_all, h_s, h_r, step)
         if step == 4:
             ring_end(h_all, h_r)
-        for stage, back in ((x_send, 0), (x_relay, 0), (z_send, 1), (last_send, 2)):
+        if step < len(STEPS):
+            x_send(step)
+            all_sent(step)
+            x_relay(step)
+        for stage, back in ((z_send, 1), (last_send, 2)):
             if 0 <= step - back < len(STEPS):
                 stage(step - back)
-
-    ring_sent(g_all, g_s)
-    ring_sent(h_all, h_s)
-    for e in NEAR_ZH:
-        for h in range(2):
-
-            def left_here():
-                sent(b_turned.at[h], bz_s.at[h, e])
-
-            if e == 0:
-                pl.when(jnp.logical_not(b_source & (core == h)))(left_here)
-            else:
-                left_here()
-
-    for i in range(2 * RZ):
-        sent(chunk(0, i), bp_s.at[i])
-
-    @pl.when(b_source)
-    def _():
-        for i in range(2 * RZ):
-            sent(chunk(0, i), bm_s.at[i])
-
-    for i in range(3):
-        sent(a_all.at[0], a_s.at[i])
-    for m in range(4):
-        sent(c_out.at[m], c_s.at[m])
-        sent(z_out.at[m], z_s.at[m])
-    for step in range(len(STEPS)):
-        n = count(step)
-        for i in range(6):
-            sent(part.at[step, 0, 0, n], x_s.at[step, i])
-        for q in range(RZ):
-            sent(x_sum.at[step, q, n], zz_s.at[step, q])
+        if step == 5:
+            steps_sent(2)
+
+    ring_sent(h_all, h_s, 3)
+    steps_sent(3)
+    steps_sent(4)
     for o in range(RY):
 
         @pl.when(owned_here(o))

time: 103 us -> 103 us (level)
  no operation moved by 1% of the time
where the time goes in v2:
time: 103 us
  Pallas kernels  101 us (98%)
  local copies, waits for them, and re-layouts  1.64 us (2%)
    pallas_call x1, Pallas kernels, body(): pl.pallas_call(kernel, out_shape=jax.ShapeDtypeStruct((ROWS, 2 * LANES),...  101 us

profile of v2, /device:TPU:3, one launch (start us, length us, event | category | flops | bytes accessed | tf_op | source)
XLA Modules:
  0.0 103.1 jit_solution(2225409952603872700)
XLA Ops:
  0.0 101.4 %shard_map.37 = bf16[448,256]{1,0:T(8,128)(2,1)} custom-call(bf16[448,896]{1,0:T(8,128)(2,1)} %a_ref.1, bf16[896,128]{1,0:T(8,128)(2,1)} %g_ref.1, bf16[128,256]{1,0:T(8,128)(2,1)} %b_ref.1), custom_call_target="tpu_custom_call" | custom-call | flops 4300000256 | bytes 2000000 | tf_op jit(solution)/shard_map/pallas_call | solution.py:421
  101.4 1.6 %copy.5 = bf16[448,256]{1,0:T(8,128)(2,1)} copy(bf16[448,256]{1,0:T(8,128)(2,1)} %shard_map.37) | data formatting | bytes 458752

commit v3 on v2

--- a/solution.py
+++ b/solution.py
@@ -379,24 +379,43 @@
             ring_sent(h_all, h_s, step - 2)
             steps_sent(step - 3)
 
-    for step in range(len(STEPS) + 2):
-        if 1 <= step <= 3:
+    def x_stage(step):
+        x_send(step)
+        all_sent(step)
+        x_relay(step)
+
+    for step in range(3):
+        if step >= 1:
             ring_hop(h_all, h_s, h_r, step)
-        if step == 4:
-            ring_end(h_all, h_r)
-        if step < len(STEPS):
-            x_send(step)
-            all_sent(step)
-            x_relay(step)
-        for stage, back in ((z_send, 1), (last_send, 2)):
-            if 0 <= step - back < len(STEPS):
-                stage(step - back)
-        if step == 5:
-            steps_sent(2)
+        x_stage(step)
+        if step >= 1:
+            z_send(step - 1)
+        if step >= 2:
+            last_send(step - 2)
+    ring_hop(h_all, h_s, h_r, 3)
+
+    def finish(order):
+        for step, before, last in zip(order, (2, order[0]), (1, 2)):
+            if step == 4:
+                ring_end(h_all, h_r)
+            x_stage(step)
+            z_send(before)
+            last_send(last)
+        z_send(order[1])
+        last_send(order[0])
+        last_send(order[1])
+
+    @pl.when(rem(y, 4) == 0)
+    def _():
+        finish((4, 3))
+
+    @pl.when(rem(y, 4) != 0)
+    def _():
+        finish((3, 4))
 
     ring_sent(h_all, h_s, 3)
-    steps_sent(3)
-    steps_sent(4)
+    for step in range(2, 5):
+        steps_sent(step)
     for o in range(RY):
 
         @pl.when(owned_here(o))

time: 103 us -> 103 us (level)
  the two profiles are of different devices: /device:TPU:3 before, /device:TPU:131 now
where the time goes in v3:
time: 103 us
  Pallas kernels  101 us (98%)
  local copies, waits for them, and re-layouts  1.64 us (2%)
    pallas_call x1, Pallas kernels, body(): pl.pallas_call(kernel, out_shape=jax.ShapeDtypeStruct((ROWS, 2 * LANES),...  101 us

profile of v3, /device:TPU:131, one launch (start us, length us, event | category | flops | bytes accessed | tf_op | source)
XLA Modules:
  0.0 102.7 jit_solution(11218200994029405933)
XLA Ops:
  0.0 101.1 %shard_map.37 = bf16[448,256]{1,0:T(8,128)(2,1)} custom-call(bf16[448,896]{1,0:T(8,128)(2,1)} %a_ref.1, bf16[896,128]{1,0:T(8,128)(2,1)} %g_ref.1, bf16[128,256]{1,0:T(8,128)(2,1)} %b_ref.1), custom_call_target="tpu_custom_call" | custom-call | flops 4300000256 | bytes 2000000 | tf_op jit(solution)/shard_map/pallas_call | solution.py:440
  101.1 1.6 %copy.5 = bf16[448,256]{1,0:T(8,128)(2,1)} copy(bf16[448,256]{1,0:T(8,128)(2,1)} %shard_map.37) | data formatting | bytes 458752

commit v4 on v2

--- a/solution.py
+++ b/solution.py
@@ -10,10 +10,11 @@
 F32 = jnp.float32
 RY, RX, RZ = 8, 4, 4
 ROWS, HALF, QUARTER, LANES = 448, 224, 112, 128
-STEPS = ((0,), (7, 1), (6, 2), (5, 3), (4,))
+SLOTS = ((0,), (1, 2), (3, 4), (5, 6), (7,))
 NEAR_Z = (0, 1, 7, 2, 6, 3, 5, 4)
 NEAR_ZH = (0, 1, 3, 2)
 FAR_FIRST = ((0, 0), (1, 2), (0, 1), (1, 3), (0, 2), (1, 0), (0, 3), (1, 1))
+AS_MADE = ((0, 0), (1, 0), (0, 1), (1, 1), (0, 2), (1, 2), (0, 3), (1, 3))
 
 
 def rem(a, b):
@@ -114,8 +115,8 @@
         owner = rem(y + (RY - hop - 1 if way == 0 else hop + 1), RY)
         arrived(ring_part(buf, owner, i), r.at[way, hop, i])
 
-    def ring_hop(buf, s, r, hop):
-        for way, i in FAR_FIRST:
+    def ring_hop(buf, s, r, hop, parts=FAR_FIRST):
+        for way, i in parts:
             ring_wait(buf, r, way, hop - 1, i)
             if hop < 3 or i // 2 == way:
                 ring_send(buf, s, r, way, hop, i)
@@ -224,8 +225,19 @@
         ).astype(BF16)
         for way in range(2):
             ring_send(h_all, h_s, h_r, way, 0, m)
+    ring_hop(h_all, h_s, h_r, 1, AS_MADE[:2])
     arrived(a_all.at[2 * zl + 1 - core], a_r.at[1])
     arrived(a_all.at[2 * (1 - zl) + 1 - core], a_r.at[2])
+
+    order = rem(y, 4)
+    last = jnp.where(order == 0, 3, jnp.where(order == 3, 4, 5))
+    steps = (
+        (0,),
+        (7, 1),
+        (6, 2),
+        (jnp.where((order == 0) | (order == 3), 5, 3), jnp.where(order == 3, 3, 4)),
+        (last,),
+    )
 
     def owner_x(o, plane):
         yy = rem(y + o, RY)
@@ -236,7 +248,7 @@
         return 2 * (1 - rem(away, 2)) + div(away, 2)
 
     def multiply(step, s):
-        offsets = STEPS[step]
+        offsets = steps[step]
         right = jnp.concatenate([h_all[rem(y + o, RY)] for o in offsets], axis=1)
         product = jnp.dot(a_all[s], right, preferred_element_type=F32).astype(BF16)
         for i, o in enumerate(offsets):
@@ -245,20 +257,20 @@
                 part[step, to_x, half, i] = product[half * HALF : (half + 1) * HALF, i * LANES : (i + 1) * LANES]
 
     def count(step):
-        return pl.ds(0, len(STEPS[step]))
+        return pl.ds(0, len(SLOTS[step]))
 
     s_up, s_down, s_far = rem(x + 1, RX), rem(x + RX - 1, RX), rem(x + 2, RX)
 
     def x_send(step):
         n = count(step)
-        if len(STEPS[step]) == 1:
-            o = STEPS[step][0]
+        if len(SLOTS[step]) == 1:
+            o = steps[step][0]
             multiply(step, rows_at(o, s_far))
         else:
             lax.fori_loop(0, 4, lambda i, carry: (multiply(step, i), carry)[1], 0)
         send(part.at[step, s_far, 0, n], relayed.at[step, 0, n], x_s.at[step, 0], rel_r.at[step, 0], x_down)
         send(part.at[step, s_far, 1, n], relayed.at[step, 1, n], x_s.at[step, 1], rel_r.at[step, 1], x_up)
-        if len(STEPS[step]) == 1:
+        if len(SLOTS[step]) == 1:
             lax.fori_loop(3, 6, lambda i, carry: (multiply(step, rows_at(o, rem(x + i, RX))), carry)[1], 0)
         send(part.at[step, s_down, 1, n], x_in.at[step, 0, 1, n], x_s.at[step, 2], x_r.at[step, 0, 1], x_down)
         send(part.at[step, s_up, 0, n], x_in.at[step, 1, 0, n], x_s.at[step, 3], x_r.at[step, 1, 0], x_up)
@@ -267,7 +279,7 @@
         n = count(step)
         for half, s, to in ((0, s_down, x_down), (1, s_up, x_up)):
             arrived(relayed.at[step, half, n], rel_r.at[step, half])
-            for i in range(len(STEPS[step])):
+            for i in range(len(SLOTS[step])):
                 part[step, s, half, i] = (
                     part[step, s, half, i].astype(F32) + relayed[step, half, i].astype(F32)
                 ).astype(BF16)
@@ -281,7 +293,7 @@
         for half in range(2):
             for side in range(2):
                 arrived(x_in.at[step, side, half, n], x_r.at[step, side, half])
-            for i in range(len(STEPS[step])):
+            for i in range(len(SLOTS[step])):
                 total = (
                     part[step, x, half, i].astype(F32)
                     + x_in[step, 0, half, i].astype(F32)
@@ -311,21 +323,21 @@
         n = count(step)
         for s in range(RZ):
             arrived(z_part.at[step, s, n], zz_r.at[step, s])
-        for i, o in enumerate(STEPS[step]):
+        for i, (slot, o) in enumerate(zip(SLOTS[step], steps[step])):
             total = z_part[step, 0, i].astype(F32)
             for s in range(1, RZ):
                 total = total + z_part[step, s, i].astype(F32)
-            z_sum[o] = total.astype(BF16)
+            z_sum[slot] = total.astype(BF16)
             to_zl, to_core, to_x, to_zh = owner(o)
 
             @pl.when(owned_here(o))
             def _():
-                pltpu.make_async_copy(z_sum.at[o], piece(core, zh), last_s.at[o]).start()
+                pltpu.make_async_copy(z_sum.at[slot], piece(core, zh), last_s.at[slot]).start()
 
             @pl.when(jnp.logical_not(owned_here(o)))
             def _():
                 send(
-                    z_sum.at[o], piece(core, zh), last_s.at[o], last_r.at[core, zh],
+                    z_sum.at[slot], piece(core, zh), last_s.at[slot], last_r.at[core, zh],
                     device(zl_=to_zl, core_=to_core, x_=to_x, zh_=to_zh),
                 )
 
@@ -379,17 +391,17 @@
             ring_sent(h_all, h_s, step - 2)
             steps_sent(step - 3)
 
-    for step in range(len(STEPS) + 2):
-        if 1 <= step <= 3:
-            ring_hop(h_all, h_s, h_r, step)
-        if step == 4:
+    for step in range(len(SLOTS) + 2):
+        if step == 3:
             ring_end(h_all, h_r)
-        if step < len(STEPS):
+        if step < len(SLOTS):
             x_send(step)
+            if step < 3:
+                ring_hop(h_all, h_s, h_r, step + 1, AS_MADE[2 if step == 0 else 0 :])
             all_sent(step)
             x_relay(step)
         for stage, back in ((z_send, 1), (last_send, 2)):
-            if 0 <= step - back < len(STEPS):
+            if 0 <= step - back < len(SLOTS):
                 stage(step - back)
         if step == 5:
             steps_sent(2)
@@ -397,15 +409,15 @@
     ring_sent(h_all, h_s, 3)
     steps_sent(3)
     steps_sent(4)
-    for o in range(RY):
+    for slot, o in enumerate(o for offsets in steps for o in offsets):
 
         @pl.when(owned_here(o))
         def _():
-            pltpu.make_async_copy(z_sum.at[o], piece(core, zh), last_s.at[o]).wait()
+            pltpu.make_async_copy(z_sum.at[slot], piece(core, zh), last_s.at[slot]).wait()
 
         @pl.when(jnp.logical_not(owned_here(o)))
         def _():
-            sent(z_sum.at[o], last_s.at[o])
+            sent(z_sum.at[slot], last_s.at[slot])
 
     for half in range(2):
         for q in range(RZ):

time: 103 us -> 102 us (level)
  Pallas kernels: 101 us -> 99.9 us
    pallas_call x1, Pallas kernels: 101 us -> 99.9 us  [body(): pl.pallas_call(kernel, out_shape=jax.ShapeDtypeStruct((ROWS, 2 * LANES),...]
where the time goes in v4:
time: 102 us
  Pallas kernels  99.9 us (98%)
  local copies, waits for them, and re-layouts  1.64 us (2%)
    pallas_call x1, Pallas kernels, body(): pl.pallas_call(kernel, out_shape=jax.ShapeDtypeStruct((ROWS, 2 * LANES),...  99.9 us

profile of v4, /device:TPU:3, one launch (start us, length us, event | category | flops | bytes accessed | tf_op | source)
XLA Modules:
  0.0 101.5 jit_solution(8706923759802693531)
XLA Ops:
  0.0 99.9 %shard_map.37 = bf16[448,256]{1,0:T(8,128)(2,1)} custom-call(bf16[448,896]{1,0:T(8,128)(2,1)} %a_ref.1, bf16[896,128]{1,0:T(8,128)(2,1)} %g_ref.1, bf16[128,256]{1,0:T(8,128)(2,1)} %b_ref.1), custom_call_target="tpu_custom_call" | custom-call | flops 4300000256 | bytes 2000000 | tf_op jit(solution)/shard_map/pallas_call | solution.py:433
  99.9 1.6 %copy.5 = bf16[448,256]{1,0:T(8,128)(2,1)} copy(bf16[448,256]{1,0:T(8,128)(2,1)} %shard_map.37) | data formatting | bytes 458752

commit v5 on v4

--- a/solution.py
+++ b/solution.py
@@ -10,7 +10,7 @@
 F32 = jnp.float32
 RY, RX, RZ = 8, 4, 4
 ROWS, HALF, QUARTER, LANES = 448, 224, 112, 128
-SLOTS = ((0,), (1, 2), (3, 4), (5, 6), (7,))
+SLOTS = ((0,), (1, 2), (3, 4), (5,), (6,), (7,))
 NEAR_Z = (0, 1, 7, 2, 6, 3, 5, 4)
 NEAR_ZH = (0, 1, 3, 2)
 FAR_FIRST = ((0, 0), (1, 2), (0, 1), (1, 3), (0, 2), (1, 0), (0, 3), (1, 1))
@@ -69,6 +69,8 @@
     for load in loads:
         load.start()
     barrier = pltpu.get_barrier_semaphore()
+    for to in (*y_to, x_up, x_down):
+        pl.semaphore_signal(barrier, inc=1, device_id=to, device_id_type=MESH)
     place = (zh * 2 + zl) * 2 + core
     for step in range(1, 16):
         there = rem(place + step, 16)
@@ -78,8 +80,6 @@
             device_id=device(zl_=rem(div(there, 2), 2), core_=rem(there, 2), zh_=div(there, 4)),
             device_id_type=MESH,
         )
-    for to in (*y_to, x_up, x_down):
-        pl.semaphore_signal(barrier, inc=1, device_id=to, device_id_type=MESH)
     from_zl = 1 - rem(div(x, 2) + rem(zh, 2), 2)
     from_x = rem(x + 2 * core + 1 - zl, RX)
 
@@ -230,13 +230,13 @@
     arrived(a_all.at[2 * (1 - zl) + 1 - core], a_r.at[2])
 
     order = rem(y, 4)
-    last = jnp.where(order == 0, 3, jnp.where(order == 3, 4, 5))
     steps = (
         (0,),
         (7, 1),
         (6, 2),
-        (jnp.where((order == 0) | (order == 3), 5, 3), jnp.where(order == 3, 3, 4)),
-        (last,),
+        (jnp.where(order == 0, 4, jnp.where(order == 3, 5, 3)),),
+        (jnp.where(order == 0, 5, jnp.where(order == 3, 3, 4)),),
+        (jnp.where(order == 0, 3, jnp.where(order == 3, 4, 5)),),
     )
 
     def owner_x(o, plane):
@@ -388,7 +388,8 @@
         elif step == 2:
             a_sent()
         else:
-            ring_sent(h_all, h_s, step - 2)
+            if step < 5:
+                ring_sent(h_all, h_s, step - 2)
             steps_sent(step - 3)
 
     for step in range(len(SLOTS) + 2):
@@ -403,12 +404,10 @@
         for stage, back in ((z_send, 1), (last_send, 2)):
             if 0 <= step - back < len(SLOTS):
                 stage(step - back)
-        if step == 5:
-            steps_sent(2)
 
     ring_sent(h_all, h_s, 3)
-    steps_sent(3)
-    steps_sent(4)
+    for step in range(3, 6):
+        steps_sent(step)
     for slot, o in enumerate(o for offsets in steps for o in offsets):
 
         @pl.when(owned_here(o))
@@ -447,11 +446,11 @@
             vmem((4, HALF, LANES), BF16),
             vmem((4, HALF, LANES), BF16),
             vmem((RY, 2 * ROWS, LANES), BF16),
-            vmem((5, 4, 2, 2, HALF, LANES), BF16),
-            vmem((5, 2, 2, HALF, LANES), BF16),
-            vmem((5, 2, 2, 2, HALF, LANES), BF16),
-            vmem((5, RZ, 2, QUARTER, LANES), BF16),
-            vmem((5, RZ, 2, QUARTER, LANES), BF16),
+            vmem((6, 4, 2, 2, HALF, LANES), BF16),
+            vmem((6, 2, 2, HALF, LANES), BF16),
+            vmem((6, 2, 2, 2, HALF, LANES), BF16),
+            vmem((6, RZ, 2, QUARTER, LANES), BF16),
+            vmem((6, RZ, 2, QUARTER, LANES), BF16),
             vmem((RY, QUARTER, LANES), BF16),
             dma((4,)),
             dma((2, 4, 4)), dma((2, 4, 4)),
@@ -462,8 +461,8 @@
             dma((3,)), dma((3,)),
             dma((4,)), dma((4,)),
             dma((4,)), dma((4,)),
-            dma((5, 6)), dma((5, 2)), dma((5, 2, 2)),
-            dma((5, RZ)), dma((5, RZ)),
+            dma((6, 6)), dma((6, 2)), dma((6, 2, 2)),
+            dma((6, RZ)), dma((6, RZ)),
             dma((RY,)), dma((2, RZ)),
         ],
         compiler_params=pltpu.CompilerParams(

time: 102 us -> 102 us (level)
  the two profiles are of different devices: /device:TPU:3 before, /device:TPU:24 now
where the time goes in v5:
time: 102 us
  Pallas kernels  100 us (98%)
  local copies, waits for them, and re-layouts  1.64 us (2%)
    pallas_call x1, Pallas kernels, body(): pl.pallas_call(kernel, out_shape=jax.ShapeDtypeStruct((ROWS, 2 * LANES),...  100 us

profile of v5, /device:TPU:24, one launch (start us, length us, event | category | flops | bytes accessed | tf_op | source)
XLA Modules:
  0.0 101.8 jit_solution(8797040093711443741)
XLA Ops:
  0.0 100.2 %shard_map.37 = bf16[448,256]{1,0:T(8,128)(2,1)} custom-call(bf16[448,896]{1,0:T(8,128)(2,1)} %a_ref.1, bf16[896,128]{1,0:T(8,128)(2,1)} %g_ref.1, bf16[128,256]{1,0:T(8,128)(2,1)} %b_ref.1), custom_call_target="tpu_custom_call" | custom-call | flops 4300000256 | bytes 2000000 | tf_op jit(solution)/shard_map/pallas_call | solution.py:432
  100.2 1.6 %copy.5 = bf16[448,256]{1,0:T(8,128)(2,1)} copy(bf16[448,256]{1,0:T(8,128)(2,1)} %shard_map.37) | data formatting | bytes 458752

commit v6 on v4

--- a/solution.py
+++ b/solution.py
@@ -131,8 +131,16 @@
             if hop < 3 or i // 2 == way:
                 sent(ring_part(buf, 0, i), s.at[way, hop, i])
 
-    for way, i in FAR_FIRST:
-        ring_send(g_all, g_s, g_r, way, 0, i)
+    def g_start(k):
+        for way, i in FAR_FIRST[2 * k - 2 : 2 * k] if k > 0 else ():
+            sent(ring_part(g_all, 0, i), g_s.at[way, 0, i])
+        for way, i in FAR_FIRST[2 * k : 2 * k + 2]:
+            ring_send(g_all, g_s, g_r, way, 0, i)
+
+    def g_step(hop, k):
+        ring_hop(g_all, g_s, g_r, hop, FAR_FIRST[2 * k : 2 * k + 2])
+
+    g_start(0)
 
     b_here = rem(x, 2) * 4
     b_zl = div(x, 2)
@@ -184,15 +192,30 @@
                 arrived(block, bm_r.at[i])
                 send(block, block, bp_s.at[i], bp_r.at[i], x_pair)
 
-    b_start(0, 3)
+    for i in range(3):
+        g_start(i + 1)
+        b_start(i, i + 1)
+    g_start(4)
     ring_hop(g_all, g_s, g_r, 1)
-    b_start(3, 8)
+    b_start(3, 4)
     send(a_all.at[own], a_all.at[own], a_s.at[0], a_r.at[0], zl_other)
     send(a_all.at[own], a_all.at[own], a_s.at[1], a_r.at[1], core_other)
-    b_forward(0, 3)
-    ring_hop(g_all, g_s, g_r, 2)
-    b_forward(3, 8)
-    ring_hop(g_all, g_s, g_r, 3)
+    b_forward(0, 2)
+    g_step(2, 0)
+    b_start(4, 5)
+    b_forward(2, 3)
+    g_step(2, 1)
+    b_start(5, 6)
+    g_step(2, 2)
+    b_start(6, 7)
+    b_forward(3, 4)
+    g_step(2, 3)
+    b_start(7, 8)
+    b_forward(4, 5)
+    for k in range(3):
+        g_step(3, k)
+        b_forward(5 + k, 6 + k)
+    g_step(3, 3)
     ring_end(g_all, g_r)
     for i in range(2 * RZ):
         arrived(chunk(4 - b_first, i), bp_r.at[i])
@@ -342,7 +365,7 @@
                 )
 
     def g_sent():
-        for hop in range(4):
+        for hop in range(1, 4):
             ring_sent(g_all, g_s, hop)
 
     def b_sent():

time: 102 us -> 103 us (level)
  Pallas kernels: 99.9 us -> 102 us
    pallas_call x1, Pallas kernels: 99.9 us -> 102 us  [body(): pl.pallas_call(kernel, out_shape=jax.ShapeDtypeStruct((ROWS, 2 * LANES),...]
where the time goes in v6:
time: 103 us
  Pallas kernels  102 us (99%)
  local copies, waits for them, and re-layouts  1.64 us (2%)
    pallas_call x1, Pallas kernels, body(): pl.pallas_call(kernel, out_shape=jax.ShapeDtypeStruct((ROWS, 2 * LANES),...  102 us

profile of v6, /device:TPU:3, one launch (start us, length us, event | category | flops | bytes accessed | tf_op | source)
XLA Modules:
  0.0 103.2 jit_solution(2433756239228080698)
XLA Ops:
  0.0 101.6 %shard_map.37 = bf16[448,256]{1,0:T(8,128)(2,1)} custom-call(bf16[448,896]{1,0:T(8,128)(2,1)} %a_ref.1, bf16[896,128]{1,0:T(8,128)(2,1)} %g_ref.1, bf16[128,256]{1,0:T(8,128)(2,1)} %b_ref.1), custom_call_target="tpu_custom_call" | custom-call | flops 4300000256 | bytes 2000000 | tf_op jit(solution)/shard_map/pallas_call | solution.py:456
  101.6 1.6 %copy.5 = bf16[448,256]{1,0:T(8,128)(2,1)} copy(bf16[448,256]{1,0:T(8,128)(2,1)} %shard_map.37) | data formatting | bytes 458752

commit v7 on v4

--- a/solution.py
+++ b/solution.py
@@ -69,6 +69,8 @@
     for load in loads:
         load.start()
     barrier = pltpu.get_barrier_semaphore()
+    for to in (*y_to, x_up, x_down):
+        pl.semaphore_signal(barrier, inc=1, device_id=to, device_id_type=MESH)
     place = (zh * 2 + zl) * 2 + core
     for step in range(1, 16):
         there = rem(place + step, 16)
@@ -78,8 +80,6 @@
             device_id=device(zl_=rem(div(there, 2), 2), core_=rem(there, 2), zh_=div(there, 4)),
             device_id_type=MESH,
         )
-    for to in (*y_to, x_up, x_down):
-        pl.semaphore_signal(barrier, inc=1, device_id=to, device_id_type=MESH)
     from_zl = 1 - rem(div(x, 2) + rem(zh, 2), 2)
     from_x = rem(x + 2 * core + 1 - zl, RX)
 
@@ -235,7 +235,7 @@
         (0,),
         (7, 1),
         (6, 2),
-        (jnp.where((order == 0) | (order == 3), 5, 3), jnp.where(order == 3, 3, 4)),
+        (jnp.where(order == 0, 4, jnp.where(order == 3, 5, 3)), jnp.where(order == 0, 5, jnp.where(order == 3, 3, 4))),
         (last,),
     )
 
@@ -263,15 +263,19 @@
 
     def x_send(step):
         n = count(step)
-        if len(SLOTS[step]) == 1:
-            o = steps[step][0]
-            multiply(step, rows_at(o, s_far))
-        else:
-            lax.fori_loop(0, 4, lambda i, carry: (multiply(step, i), carry)[1], 0)
+        s_first = rows_at(steps[step][0], s_far)
+        s_next = rows_at(steps[step][-1], s_far)
+        s_next = jnp.where(s_next == s_first, rows_at(steps[step][0], s_down), s_next)
+        s_third = rem(s_first + 1, 4)
+        s_third = jnp.where(s_third == s_next, rem(s_first + 2, 4), s_third)
+        rows = (s_first, s_next, s_third, 6 - s_first - s_next - s_third)
+        early = len(SLOTS[step])
+        for s in rows[:early]:
+            multiply(step, s)
         send(part.at[step, s_far, 0, n], relayed.at[step, 0, n], x_s.at[step, 0], rel_r.at[step, 0], x_down)
         send(part.at[step, s_far, 1, n], relayed.at[step, 1, n], x_s.at[step, 1], rel_r.at[step, 1], x_up)
-        if len(SLOTS[step]) == 1:
-            lax.fori_loop(3, 6, lambda i, carry: (multiply(step, rows_at(o, rem(x + i, RX))), carry)[1], 0)
+        for s in rows[early:]:
+            multiply(step, s)
         send(part.at[step, s_down, 1, n], x_in.at[step, 0, 1, n], x_s.at[step, 2], x_r.at[step, 0, 1], x_down)
         send(part.at[step, s_up, 0, n], x_in.at[step, 1, 0, n], x_s.at[step, 3], x_r.at[step, 1, 0], x_up)
 

time: 102 us -> 100 us (0.980)
  the two profiles are of different devices: /device:TPU:3 before, /device:TPU:89 now
where the time goes in v7:
time: 100 us
  Pallas kernels  98.6 us (99%)
  local copies, waits for them, and re-layouts  1.64 us (2%)
    pallas_call x1, Pallas kernels, body(): pl.pallas_call(kernel, out_shape=jax.ShapeDtypeStruct((ROWS, 2 * LANES),...  98.6 us

profile of v7, /device:TPU:89, one launch (start us, length us, event | category | flops | bytes accessed | tf_op | source)
XLA Modules:
  0.0 100.3 jit_solution(7573483917181098028)
XLA Ops:
  0.0 98.6 %shard_map.37 = bf16[448,256]{1,0:T(8,128)(2,1)} custom-call(bf16[448,896]{1,0:T(8,128)(2,1)} %a_ref.1, bf16[896,128]{1,0:T(8,128)(2,1)} %g_ref.1, bf16[128,256]{1,0:T(8,128)(2,1)} %b_ref.1), custom_call_target="tpu_custom_call" | custom-call | flops 4300000256 | bytes 2000000 | tf_op jit(solution)/shard_map/pallas_call | solution.py:437
  98.6 1.6 %copy.5 = bf16[448,256]{1,0:T(8,128)(2,1)} copy(bf16[448,256]{1,0:T(8,128)(2,1)} %shard_map.37) | data formatting | bytes 458752

commit v8 on v7

--- a/solution.py
+++ b/solution.py
@@ -269,15 +269,19 @@
         s_third = rem(s_first + 1, 4)
         s_third = jnp.where(s_third == s_next, rem(s_first + 2, 4), s_third)
         rows = (s_first, s_next, s_third, 6 - s_first - s_next - s_third)
-        early = len(SLOTS[step])
+        early, late = len(SLOTS[step]), 4
+        if early == 1:
+            rows, late = tuple(rows_at(steps[step][0], to_x) for to_x in (s_far, s_down, s_up, x)), 3
         for s in rows[:early]:
             multiply(step, s)
         send(part.at[step, s_far, 0, n], relayed.at[step, 0, n], x_s.at[step, 0], rel_r.at[step, 0], x_down)
         send(part.at[step, s_far, 1, n], relayed.at[step, 1, n], x_s.at[step, 1], rel_r.at[step, 1], x_up)
-        for s in rows[early:]:
+        for s in rows[early:late]:
             multiply(step, s)
         send(part.at[step, s_down, 1, n], x_in.at[step, 0, 1, n], x_s.at[step, 2], x_r.at[step, 0, 1], x_down)
         send(part.at[step, s_up, 0, n], x_in.at[step, 1, 0, n], x_s.at[step, 3], x_r.at[step, 1, 0], x_up)
+        for s in rows[late:]:
+            multiply(step, s)
 
     def x_relay(step):
         n = count(step)

time: 100 us -> 100 us (level)
  the two profiles are of different devices: /device:TPU:89 before, /device:TPU:3 now
where the time goes in v8:
time: 100 us
  Pallas kernels  98.3 us (98%)
  local copies, waits for them, and re-layouts  1.64 us (2%)
    pallas_call x1, Pallas kernels, body(): pl.pallas_call(kernel, out_shape=jax.ShapeDtypeStruct((ROWS, 2 * LANES),...  98.3 us

profile of v8, /device:TPU:3, one launch (start us, length us, event | category | flops | bytes accessed | tf_op | source)
XLA Modules:
  0.0 100.0 jit_solution(6290605372307911065)
XLA Ops:
  0.0 98.3 %shard_map.37 = bf16[448,256]{1,0:T(8,128)(2,1)} custom-call(bf16[448,896]{1,0:T(8,128)(2,1)} %a_ref.1, bf16[896,128]{1,0:T(8,128)(2,1)} %g_ref.1, bf16[128,256]{1,0:T(8,128)(2,1)} %b_ref.1), custom_call_target="tpu_custom_call" | custom-call | flops 4300000256 | bytes 2000000 | tf_op jit(solution)/shard_map/pallas_call | solution.py:441
  98.3 1.6 %copy.5 = bf16[448,256]{1,0:T(8,128)(2,1)} copy(bf16[448,256]{1,0:T(8,128)(2,1)} %shard_map.37) | data formatting | bytes 458752
